TPU v7x, 32 devices: a whole 2x2x4 slice. The times are simulated.
32 devices in a mesh: wide: 8 (over z, y), narrow: 4 (over x, core).
Axes of the slice: x: 2, y: 2, z: 4, core: 2. Of those that a mesh axis runs over, the one named last changes fastest.
Arguments:
- byte_ids: int32 [32, 1488], P(('wide', 'narrow')), may hold values from 0 to 258
- lengths: int32 [32, 2], P(('wide', 'narrow')), may hold values from 186 to 744, as said below
- bucket: int32 [32], P(('wide', 'narrow')), may hold values 0 or 1
- out_grad: bfloat16 [32, 744, 768], P(('wide', 'narrow')), may hold values from -6 to 6
- embedding: bfloat16 [259, 768], P(None, 'wide')
- score_weight: bfloat16 [768], P('wide'), may hold values from -0.625 to 0.625
- gain_attn: bfloat16 [768], P('wide'), may hold values from 0.5 to 1.5
- w_query: bfloat16 [768, 768], P('wide'), may hold values from -0.02734375 to 0.02734375
- w_key: bfloat16 [768, 768], P('wide'), may hold values from -0.21875 to 0.21875
- w_value: bfloat16 [768, 768], P('wide'), may hold values from -0.21875 to 0.21875
- w_attn_out: bfloat16 [768, 768], P('wide'), may hold values from -0.875 to 0.875
- rel_bias: bfloat16 [32, 12], replicated, may hold values from -3 to 3
- gain_ff: bfloat16 [768], P('wide'), may hold values from 0.5 to 1.5
- w_gate: bfloat16 [768, 2048], P('wide'), may hold values from -0.21875 to 0.21875
- w_up: bfloat16 [768, 2048], P('wide'), may hold values from -0.21875 to 0.21875
- w_ff_out: bfloat16 [2048, 768], P('wide'), may hold values from -0.125 to 0.125
Outputs:
- encoded: bfloat16 [32, 744, 768], P(('wide', 'narrow'))
- grad_embedding: float32 [259, 768], P(None, 'wide')
- grad_score_weight: float32 [768], P('wide')
- grad_gain_attn: float32 [768], P('wide')
- grad_w_query: float32 [768, 768], P('wide')
- grad_w_key: float32 [768, 768], P('wide')
- grad_w_value: float32 [768, 768], P('wide')
- grad_w_attn_out: float32 [768, 768], P('wide')
- grad_rel_bias: float32 [32, 12], replicated
- grad_gain_ff: float32 [768], P('wide')
- grad_w_gate: float32 [768, 2048], P('wide')
- grad_w_up: float32 [768, 2048], P('wide')
- grad_w_ff_out: float32 [2048, 768], P('wide')
- block_share: float32 [4], replicated
Inputs may be any that keep to these rules, and one draw needn't show every extreme that they name: Where bucket is 0 a group holds two sequences of lengths[g,0] and lengths[g,1] bytes in its two slots; where it is 1, one sequence of lengths[g,0] + lengths[g,1] bytes from the group's first byte. Some entry equals 744 and some equals 186.
All inputs are finite; a program needn't handle non-finite values. No bound on the sum of `bucket` on one device may be relied on, other than what follows from the above.
Results may differ from a plain program's by a relative error of at most 0.012.
Values may be sent and summed in bfloat16 or wider, within the bound.
A program may use at most 256 MiB of HBM per device.

v0:
```python
import jax
import jax.numpy as jnp
from jax import lax
from jax.sharding import PartitionSpec as P

highest = lax.Precision.HIGHEST
thresholds = (12, 16, 23, 32, 46, 64, 91)
epsilon = 1e-06
block_sizes = (1, 2, 3, 4)


def bucket_of(relative):
    distance = jnp.abs(relative)
    far_bucket = 8 + sum(
        ((distance >= threshold_edge).astype(jnp.int32) for threshold_edge in thresholds)
    )
    near_far = jnp.where(distance < 8, distance, far_bucket)
    return near_far + 16 * (relative > 0).astype(jnp.int32)


def valid_masks(length_pair, joined_flag, slot_bytes):
    position = jnp.arange(2 * slot_bytes, dtype=jnp.int32)
    in_slot = position % slot_bytes
    slot_limit = jnp.where(position < slot_bytes, length_pair[0], length_pair[1])
    joined = joined_flag == 1
    byte_valid = jnp.where(joined, position < length_pair[0] + length_pair[1], in_slot < slot_limit)
    token_index = jnp.arange(slot_bytes, dtype=jnp.int32)
    segment = jnp.where(joined, 0, token_index // (slot_bytes // 2))
    token_valid = byte_valid[0::2]
    attend = (segment[:, None] == segment[None, :]) & token_valid[None, :]
    return (byte_valid.astype(jnp.float32), attend)


def gbst_mix(embedded, byte_valid, score_vector):
    nbytes, model_width = embedded.shape
    tile_count = nbytes // 12
    masked = (embedded * byte_valid[:, None]).reshape(tile_count, 12, model_width)
    counted = byte_valid.reshape(tile_count, 12)
    spread_blocks = []
    block_scores = []
    for block_size in block_sizes:
        groups_here = 12 // block_size
        summed = jnp.sum(masked.reshape(tile_count, groups_here, block_size, model_width), axis=2)
        members = jnp.maximum(
            jnp.sum(counted.reshape(tile_count, groups_here, block_size), axis=2), 1.0
        )
        pooled = summed / members[..., None]
        rating = jnp.sum(pooled * score_vector, axis=-1)
        spread_blocks.append(
            jnp.broadcast_to(
                pooled[:, :, None, :], (tile_count, groups_here, block_size, model_width)
            ).reshape(nbytes, model_width)
        )
        block_scores.append(
            jnp.broadcast_to(rating[:, :, None], (tile_count, groups_here, block_size)).reshape(
                nbytes
            )
        )
    block_weights = jax.nn.softmax(jnp.stack(block_scores), axis=0)
    mixed = sum(
        (block_weights[size_index][:, None] * spread_blocks[size_index] for size_index in range(4))
    )
    stream = jnp.mean(mixed.reshape(nbytes // 2, 2, model_width), axis=1)
    return (stream, block_weights)


def rms_scale(activations, gain_vector):
    return (
        activations
        * lax.rsqrt(jnp.mean(activations * activations, axis=-1, keepdims=True) + epsilon)
        * gain_vector
    )


def gelu_gate(gate_in, up_in):
    return jax.nn.gelu(gate_in, approximate=True) * up_in


def plain_product(left, right):
    return jnp.dot(left, right, preferred_element_type=jnp.float32)


def rows_product(left, right):
    return lax.dot_general(
        left, right, (((1,), (1,)), ((), ())), preferred_element_type=jnp.float32
    )


def columns_product(left, right):
    return lax.dot_general(
        left, right, (((0,), (0,)), ((), ())), preferred_element_type=jnp.float32
    )


def relative_matrix(vector, length):
    tiled = jnp.tile(vector, length + 1)
    flattened = lax.slice(tiled, (length - 1,), (length - 1 + length * (2 * length - 2),))
    return flattened.reshape(length, 2 * length - 2)[:, :length]


def diagonal_totals(matrix, length):
    padded_rows = jnp.pad(matrix, ((0, 0), (0, length - 2)))
    flattened = padded_rows.reshape(-1)
    trailing = (length + 1) * (2 * length - 1) - (length - 1) - length * (2 * length - 2)
    flattened = jnp.pad(flattened, (length - 1, trailing))
    return jnp.sum(flattened.reshape(length + 1, 2 * length - 1), axis=0)


def body(
    byte_ids,
    lengths,
    bucket,
    out_grad,
    embedding,
    score_weight,
    gain_attn,
    w_query,
    w_key,
    w_value,
    w_attn_out,
    rel_bias,
    gain_ff,
    w_gate,
    w_up,
    w_ff_out,
):
    gathered = (
        lax.all_gather(embedding, "wide", axis=1, tiled=True),
        lax.all_gather(score_weight, "wide", axis=0, tiled=True),
        lax.all_gather(gain_attn, "wide", axis=0, tiled=True),
        lax.all_gather(w_query, "wide", axis=0, tiled=True),
        lax.all_gather(w_key, "wide", axis=0, tiled=True),
        lax.all_gather(w_value, "wide", axis=0, tiled=True),
        lax.all_gather(w_attn_out, "wide", axis=0, tiled=True),
        lax.all_gather(gain_ff, "wide", axis=0, tiled=True),
        lax.all_gather(w_gate, "wide", axis=0, tiled=True),
        lax.all_gather(w_up, "wide", axis=0, tiled=True),
        lax.all_gather(w_ff_out, "wide", axis=0, tiled=True),
    )
    (
        byte_table,
        score_full,
        gain_one,
        query_full,
        key_full,
        value_full,
        out_full,
        gain_two,
        gate_full,
        up_full,
        down_full,
    ) = gathered
    token_ids = byte_ids[0]
    slot_bytes = token_ids.shape[0] // 2
    model_width = byte_table.shape[1]
    head_count = rel_bias.shape[1]
    head_size = model_width // head_count
    vocab_size = byte_table.shape[0]
    byte_valid, attend = valid_masks(lengths[0], bucket[0], slot_bytes)
    onehot = (token_ids[:, None] == jnp.arange(vocab_size, dtype=jnp.int32)[None, :]).astype(
        jnp.bfloat16
    )
    embedded = plain_product(onehot, byte_table)
    stream, gbst_pull, block_weights = jax.vjp(
        lambda inputs, scorer: gbst_mix(inputs, byte_valid, scorer),
        embedded,
        score_full.astype(jnp.float32),
        has_aux=True,
    )
    normed_f, norm_one_pull = jax.vjp(rms_scale, stream, gain_one.astype(jnp.float32))
    normed = normed_f.astype(jnp.bfloat16)

    def split_heads(matrix):
        return matrix.reshape(slot_bytes, head_count, head_size).transpose(1, 0, 2)

    def join_heads(stacked):
        return stacked.transpose(1, 0, 2).reshape(slot_bytes, model_width)

    query_heads = split_heads(plain_product(normed, query_full).astype(jnp.bfloat16))
    key_heads = split_heads(plain_product(normed, key_full).astype(jnp.bfloat16))
    value_heads = split_heads(plain_product(normed, value_full).astype(jnp.bfloat16))
    offsets = jnp.arange(2 * slot_bytes - 1, dtype=jnp.int32) - (slot_bytes - 1)
    bucket_hot = (
        bucket_of(offsets)[:, None] == jnp.arange(rel_bias.shape[0], dtype=jnp.int32)[None, :]
    ).astype(jnp.float32)
    bias_rows = jnp.dot(bucket_hot, rel_bias.astype(jnp.float32), precision=highest).T

    def head_scores(query_head, key_head, bias_row):
        scores = rows_product(query_head, key_head) + relative_matrix(bias_row, slot_bytes)
        return jnp.where(attend, scores, -1e30)

    def head_forward(operands):
        query_head, key_head, value_head, bias_row = operands
        scores = head_scores(query_head, key_head, bias_row)
        row_peak = jnp.max(scores, axis=1, keepdims=True)
        raised = jnp.exp(scores - row_peak)
        row_total = jnp.sum(raised, axis=1, keepdims=True)
        softmax_rows = (raised / row_total).astype(jnp.bfloat16)
        return (
            plain_product(softmax_rows, value_head).astype(jnp.bfloat16),
            row_peak + jnp.log(row_total),
        )

    head_out, log_totals = lax.map(head_forward, (query_heads, key_heads, value_heads, bias_rows))
    mixed_heads = join_heads(head_out)
    middle = stream + plain_product(mixed_heads, out_full)
    normed_ff_f, norm_two_pull = jax.vjp(rms_scale, middle, gain_two.astype(jnp.float32))
    normed_ff = normed_ff_f.astype(jnp.bfloat16)
    gate_act = plain_product(normed_ff, gate_full)
    upward = plain_product(normed_ff, up_full)
    activated, glu_pull = jax.vjp(gelu_gate, gate_act, upward)
    hidden = activated.astype(jnp.bfloat16)
    result = middle + plain_product(hidden, down_full)
    encoded = result.astype(jnp.bfloat16)[None]
    again = (
        lax.all_gather(w_query, "wide", axis=0, tiled=True),
        lax.all_gather(w_key, "wide", axis=0, tiled=True),
        lax.all_gather(w_value, "wide", axis=0, tiled=True),
        lax.all_gather(w_attn_out, "wide", axis=0, tiled=True),
        lax.all_gather(w_gate, "wide", axis=0, tiled=True),
        lax.all_gather(w_up, "wide", axis=0, tiled=True),
        lax.all_gather(w_ff_out, "wide", axis=0, tiled=True),
    )
    query_back, key_back, value_back, out_back, gate_back, up_back, down_back = again
    upstream = out_grad[0]
    grad_down = columns_product(hidden, upstream)
    grad_hidden = rows_product(upstream, down_back)
    grad_gate_f, grad_up_f = glu_pull(grad_hidden)
    grad_gate_b = grad_gate_f.astype(jnp.bfloat16)
    grad_up_b = grad_up_f.astype(jnp.bfloat16)
    grad_w_gate = columns_product(normed_ff, grad_gate_b)
    grad_w_up = columns_product(normed_ff, grad_up_b)
    grad_normed_ff = rows_product(grad_gate_b, gate_back) + rows_product(grad_up_b, up_back)
    grad_middle_norm, grad_gain_two = norm_two_pull(grad_normed_ff)
    grad_middle = upstream.astype(jnp.float32) + grad_middle_norm
    grad_branch = grad_middle.astype(jnp.bfloat16)
    grad_w_out = columns_product(mixed_heads, grad_branch)
    grad_mixed = rows_product(grad_branch, out_back).astype(jnp.bfloat16)

    def head_backward(operands):
        query_head, key_head, value_head, bias_row, grad_head, log_row = operands
        scores = head_scores(query_head, key_head, bias_row)
        softmax_rows = jnp.exp(scores - log_row)
        grad_rows = rows_product(grad_head, value_head)
        inner_sum = jnp.sum(softmax_rows * grad_rows, axis=1, keepdims=True)
        grad_scores = (softmax_rows * (grad_rows - inner_sum)).astype(jnp.bfloat16)
        grad_query = plain_product(grad_scores, key_head).astype(jnp.bfloat16)
        grad_key = columns_product(grad_scores, query_head).astype(jnp.bfloat16)
        grad_value = columns_product(softmax_rows.astype(jnp.bfloat16), grad_head).astype(
            jnp.bfloat16
        )
        grad_bias = diagonal_totals(grad_scores.astype(jnp.float32), slot_bytes)
        return (grad_query, grad_key, grad_value, grad_bias)

    grad_query_heads, grad_key_heads, grad_value_heads, grad_bias_rows = lax.map(
        head_backward,
        (query_heads, key_heads, value_heads, bias_rows, split_heads(grad_mixed), log_totals),
    )
    grad_queries = join_heads(grad_query_heads)
    grad_keys = join_heads(grad_key_heads)
    grad_values = join_heads(grad_value_heads)
    grad_w_query = columns_product(normed, grad_queries)
    grad_w_key = columns_product(normed, grad_keys)
    grad_w_value = columns_product(normed, grad_values)
    grad_normed = (
        rows_product(grad_queries, query_back)
        + rows_product(grad_keys, key_back)
        + rows_product(grad_values, value_back)
    )
    grad_stream_norm, grad_gain_one = norm_one_pull(grad_normed)
    grad_stream = grad_middle + grad_stream_norm
    grad_embedded, grad_score = gbst_pull(grad_stream)
    grad_table = columns_product(onehot, grad_embedded.astype(jnp.bfloat16))
    grad_relative = jnp.dot(bucket_hot.T, grad_bias_rows.T, precision=highest)
    shares = (
        lax.psum_scatter(grad_table, "wide", scatter_dimension=1, tiled=True),
        lax.psum_scatter(grad_score, "wide", scatter_dimension=0, tiled=True),
        lax.psum_scatter(grad_gain_one, "wide", scatter_dimension=0, tiled=True),
        lax.psum_scatter(grad_w_query, "wide", scatter_dimension=0, tiled=True),
        lax.psum_scatter(grad_w_key, "wide", scatter_dimension=0, tiled=True),
        lax.psum_scatter(grad_w_value, "wide", scatter_dimension=0, tiled=True),
        lax.psum_scatter(grad_w_out, "wide", scatter_dimension=0, tiled=True),
        lax.psum_scatter(grad_gain_two, "wide", scatter_dimension=0, tiled=True),
        lax.psum_scatter(grad_w_gate, "wide", scatter_dimension=0, tiled=True),
        lax.psum_scatter(grad_w_up, "wide", scatter_dimension=0, tiled=True),
        lax.psum_scatter(grad_down, "wide", scatter_dimension=0, tiled=True),
    )
    summed = lax.psum(
        (
            shares[0],
            shares[1],
            shares[2],
            shares[3],
            shares[4],
            shares[5],
            shares[6],
            shares[7],
            shares[8],
            shares[9],
            shares[10],
        ),
        "narrow",
    )
    (
        sum_table,
        sum_score,
        sum_gain_one,
        sum_query,
        sum_key,
        sum_value,
        sum_out,
        sum_gain_two,
        sum_gate,
        sum_up,
        sum_down,
    ) = summed
    local_totals = jnp.sum(block_weights * byte_valid[None, :], axis=1)
    relative_total, block_totals, valid_total = lax.psum(
        (grad_relative, local_totals, jnp.sum(byte_valid)), ("wide", "narrow")
    )
    block_share = block_totals / valid_total
    return (
        encoded,
        sum_table,
        sum_score,
        sum_gain_one,
        sum_query,
        sum_key,
        sum_value,
        sum_out,
        relative_total,
        sum_gain_two,
        sum_gate,
        sum_up,
        sum_down,
        block_share,
    )


def solution(mesh):
    placed = (
        P(("wide", "narrow"), None),
        P(("wide", "narrow"), None),
        P(("wide", "narrow")),
        P(("wide", "narrow"), None, None),
        P(None, "wide"),
        P("wide"),
        P("wide"),
        P("wide", None),
        P("wide", None),
        P("wide", None),
        P("wide", None),
        P(),
        P("wide"),
        P("wide", None),
        P("wide", None),
        P("wide", None),
    )
    return jax.shard_map(
        body,
        mesh=mesh,
        in_specs=placed,
        out_specs=(
            P(("wide", "narrow"), None, None),
            P(None, "wide"),
            P("wide"),
            P("wide"),
            P("wide", None),
            P("wide", None),
            P("wide", None),
            P("wide", None),
            P(),
            P("wide"),
            P("wide", None),
            P("wide", None),
            P("wide", None),
            P(),
        ),
        check_vma=False,
    )
```

profile of v0, /device:TPU:0, one launch (start us, length us, event | category | flops | bytes accessed | tf_op | source)
XLA Modules:
  0.0 2359.3 jit_solution(4324857130846443131)
XLA Ops:
  24.1 23.6 all-reduce.16
  47.7 31.6 %all-gather = bf16[8,96,259]{1,2,0:T(8,128)(2,1)S(1)} all-gather(bf16[1,96,259]{1,2,0:T(8,128)(2,1)} %bitcast.189), channel_id=1, replica_groups=mesh['wide'=8,'narrow'=4] {'wide'}, dimensions={0}, use_global_device_ids=true | all-gather | bytes 447552 | tf_op jit(solution)/shard_map/all_gather | solution.py:128
  90.4 7.8 reshape.594
  107.2 7.8 reduce_sum.359
  119.3 7.9 reduce_sum.362
  163.2 9.1 reshape.601
  188.9 12.9 add_reduce_fusion
  225.7 364.2 %while.32 = (s32[]{:T(128)}, bf16[12,744,64]{1,2,0:T(8,128)(2,1)}, f32[12,744,1]{1,2,0:T(1,128)}, bf16[12,744,64]{2,1,0:T(8,128)(2,1)}, bf16[12,744,64]{2,1,0:T(...) while((s32[]{:T(128)}, bf16[12,744,64]{1,2,0:T(8,128)(2,1)}, ...), condition=%wide.region_16.17_spmd.clone, body=%wide.region_13.16_spmd.clone.sunk | while | flops 147287456 | bytes 51853992 | solution.py:204
  228.7 7.5 tile.42
  259.1 7.6 tile.42
  289.4 7.5 tile.42
  319.8 7.6 tile.42
  350.1 7.6 tile.42
  380.4 7.5 tile.42
  410.7 7.5 tile.42
  441.0 7.5 tile.42
  471.2 7.5 tile.42
  501.5 7.5 tile.42
  593.9 7.9 fusion.125
  608.8 12.6 multiply_convert_fusion.1
  637.0 777.5 %while.33 = (s32[]{:T(128)}, bf16[12,744,64]{1,2,0:T(8,128)(2,1)}, bf16[12,744,64]{1,2,0:T(8,128)(2,1)}, bf16[12,744,64]{1,2,0:T(8,128)(2,1)}, f32[12,1487]{1,0:...) while((s32[]{:T(128)}, bf16[12,744,64]{1,2,0:T(8,128)(2,1)}, ...), condition=%wide.region_22.23_spmd.clone, body=%wide.region_19.22_spmd.clone.sunk | while | flops 362708192 | bytes 101429248 | solution.py:255
  684.1 7.7 reshape.670
  748.9 7.7 reshape.670
  813.6 7.7 reshape.670
  878.4 7.7 reshape.670
  943.1 7.7 reshape.670
  1007.9 7.7 reshape.670
  1072.6 7.7 reshape.670
  1137.4 7.7 reshape.670
  1202.1 7.7 reshape.670
  1266.8 7.7 reshape.670
  1331.6 7.7 reshape.670
  1396.3 7.7 reshape.670
  1437.4 8.8 broadcast_in_dim.233
  1456.4 7.6 multiply_reduce_fusion.7
  1465.8 9.2 multiply_reduce_fusion.1
  1494.5 8.1 reshape.613
  1530.9 9.7 fusion.63
  1580.6 21.9 reduce-scatter.25.cloned.1.call-done
  1604.2 69.9 %reduce-scatter.17.cloned.1.call-done = f32[96,768]{1,0:T(8,128)} async-done(((f32[768,768]{1,0:T(8,128)}), f32[96,768]{1,0:T(8,128)}) %reduce-scatter.17.cloned.1.call-update) | async-done | bytes 294928 | tf_op jit(solution)/shard_map/reduce_scatter | solution.py:282
  1674.2 71.4 %reduce-scatter.11.cloned.1.call-done = f32[96,768]{1,0:T(8,128)} async-done(((f32[768,768]{1,0:T(8,128)}), f32[96,768]{1,0:T(8,128)}) %reduce-scatter.11.cloned.1.call-update) | async-done | bytes 294928 | tf_op jit(solution)/shard_map/reduce_scatter | solution.py:279
  1745.6 71.9 %reduce-scatter.13.cloned.1.call-done = f32[96,768]{1,0:T(8,128)} async-done(((f32[768,768]{1,0:T(8,128)}), f32[96,768]{1,0:T(8,128)}) %reduce-scatter.13.cloned.1.call-update) | async-done | bytes 294928 | tf_op jit(solution)/shard_map/reduce_scatter | solution.py:280
  1817.4 71.6 %reduce-scatter.15.cloned.1.call-done = f32[96,768]{1,0:T(8,128)} async-done(((f32[768,768]{1,0:T(8,128)}), f32[96,768]{1,0:T(8,128)}) %reduce-scatter.15.cloned.1.call-update) | async-done | bytes 294928 | tf_op jit(solution)/shard_map/reduce_scatter | solution.py:281
  1889.0 120.6 %reduce-scatter.19.cloned.1.call-done = f32[96,2048]{1,0:T(8,128)} async-done(((f32[768,2048]{1,0:T(8,128)}), f32[96,2048]{1,0:T(8,128)}) %reduce-scatter.19.cloned.1.call-update) | async-done | bytes 786448 | tf_op jit(solution)/shard_map/reduce_scatter | solution.py:284
  2009.6 120.6 %reduce-scatter.21.cloned.1.call-done = f32[96,2048]{1,0:T(8,128)} async-done(((f32[768,2048]{1,0:T(8,128)}), f32[96,2048]{1,0:T(8,128)}) %reduce-scatter.21.cloned.1.call-update) | async-done | bytes 786448 | tf_op jit(solution)/shard_map/reduce_scatter | solution.py:285
  2130.2 120.6 %reduce-scatter.23.cloned.1.call-done = f32[256,768]{1,0:T(8,128)} async-done(((f32[2048,768]{1,0:T(8,128)}), f32[256,768]{1,0:T(8,128)}) %reduce-scatter.23.cloned.1.call-update) | async-done | bytes 786448 | tf_op jit(solution)/shard_map/reduce_scatter | solution.py:286
  2253.9 35.3 %all-reduce.13 = (f32[768]{0:T(1024)S(1)}, f32[768]{0:T(1024)S(1)}, f32[768]{0:T(1024)S(1)}) all-reduce(f32[768]{0:T(1024)S(1)} %add_add_fusion.3, f32[768]{0:T(1024)S(1)} %copy-done.74, f32[768]{0:T(1024)S(1)} %copy-done.81), channel_id=3, replica_groups=mesh['wide'=8,'narrow'=4] {'wide'}, use_global_device_ids=true, to_apply=%region_41.42.clone | all-reduce | flops 2304 | bytes 18432
  2296.0 37.6 %all-reduce.12 = (f32[32,12]{0,1:T(8,128)}, f32[4]{0:T(128)S(1)}, f32[]{:T(128)}) all-reduce(f32[32,12]{0,1:T(8,128)S(1)} %fusion.71, f32[4]{0:T(128)S(1)} %copy-done.82, f32[]{:T(128)} %convert_reduce_fusion.2), channel_id=1, replica_groups=mesh['wide'=8,'narrow'=4] {'wide','narrow'}, use_global_device_ids=true, to_apply=%region_54.55 | all-reduce | flops 389 | bytes 3112 | tf_op jit(solution)/shard_map/psum | solution.py:318
  (821 shorter events, 1265.2 us)
Async XLA Ops:
  7.2 197.9 %copy-start = (bf16[32,12]{0,1:T(8,128)(2,1)S(1)}, bf16[32,12]{0,1:T(8,128)(2,1)}, u32[]{:S(2)}) copy-start(bf16[32,12]{0,1:T(8,128)(2,1)} %param.31) | copy-start | bytes 2308
  7.2 200.2 %all-gather.9.cloned.1.call-start = ((), (), s32[]{:S(2)}) async-start(), calls=%async_computation.8 | async-start | bytes 1327104 | tf_op jit(solution)/shard_map/all_gather | solution.py:131
  7.9 205.2 %all-gather.11.cloned.1.call-start = ((), (), s32[]{:S(2)}) async-start(), calls=%async_computation.9 | async-start | bytes 1327104 | tf_op jit(solution)/shard_map/all_gather | solution.py:132
  8.7 71.2 %copy-start.80 = (s32[1,1488]{1,0:T(1,128)S(1)}, s32[1,1488]{1,0:T(1,128)}, u32[]{:S(2)}) copy-start(s32[1,1488]{1,0:T(1,128)} %param.20) | copy-start | bytes 17860
  8.7 210.2 %all-gather.13.cloned.1.call-start = ((), (), s32[]{:S(2)}) async-start(), calls=%async_computation.10 | async-start | bytes 1327104 | tf_op jit(solution)/shard_map/all_gather | solution.py:133
  9.4 580.5 %all-gather.15.cloned.1.call-start = ((), (), s32[]{:S(2)}) async-start(), calls=%async_computation.11 | async-start | bytes 1327104 | tf_op jit(solution)/shard_map/all_gather | solution.py:134
  10.0 583.9 %all-gather.17.cloned.1.call-start = ((), (), s32[]{:S(2)}) async-start(), calls=%async_computation.12 | async-start | bytes 3538944 | tf_op jit(solution)/shard_map/all_gather | solution.py:136
  10.6 591.1 %all-gather.19.cloned.1.call-start = ((), (), s32[]{:S(2)}) async-start(), calls=%async_computation.13 | async-start | bytes 3538944 | tf_op jit(solution)/shard_map/all_gather | solution.py:137
  11.2 597.6 %all-gather.21.cloned.1.call-start = ((), (), s32[]{:S(2)}) async-start(), calls=%async_computation.14 | async-start | bytes 3538944 | tf_op jit(solution)/shard_map/all_gather | solution.py:138
  11.9 1590.6 %reduce-scatter.25.cloned.1.call-start = ((), (), s32[]{:S(2)}) async-start(), calls=%async_computation.22 | async-start | bytes 1327104
  17.9 134.4 %copy-start.69 = (f32[1488]{0:T(1024)}, f32[1488]{0:T(1024)S(1)}, u32[]{:S(2)}) copy-start(f32[1488]{0:T(1024)S(1)} %fusion.119) | copy-start | bytes 17860
  47.7 90.5 %copy-start.46 = (f32[768]{0:T(1024)}, f32[768]{0:T(1024)S(1)}, u32[]{:S(2)}) copy-start(f32[768]{0:T(1024)S(1)} %convert_element_type.199) | copy-start | bytes 9220
  107.2 36.4 %copy-start.34 = (f32[124,6]{1,0:T(8,128)}, f32[124,6]{1,0:T(8,128)S(1)}, u32[]{:S(2)}) copy-start(f32[124,6]{1,0:T(8,128)S(1)} %copy.74) | copy-start | bytes 8932
  115.0 26.9 %copy-start.5 = (f32[124,6,768]{2,1,0:T(8,128)}, f32[124,6,768]{2,1,0:T(8,128)S(1)}, u32[]{:S(2)}) copy-start(f32[124,6,768]{2,1,0:T(8,128)S(1)} %reduce_sum.359) | copy-start | bytes 6856708
  119.3 33.1 %copy-start.48 = (f32[1,1488]{1,0:T(1,128)}, f32[1,1488]{1,0:T(1,128)S(1)}, u32[]{:S(2)}) copy-start(f32[1,1488]{1,0:T(1,128)S(1)} %reshape.593) | copy-start | bytes 17860
  131.5 20.8 copy-start.52
  141.8 10.5 copy-start.54
  143.7 42.9 %copy-start.64 = (f32[744]{0:T(1024)}, f32[744]{0:T(1024)S(1)}, u32[]{:S(2)}) copy-start(f32[744]{0:T(1024)S(1)} %max.66) | copy-start | bytes 8932
  150.2 8.6 copy-start.7
  152.3 11.0 copy-start.44
  153.2 10.0 copy-start.71
  163.2 9.1 copy-start.9
  175.2 11.4 copy-start.11
  593.5 35.4 %copy-start.21 = (f32[744,768]{1,0:T(8,128)}, f32[744,768]{1,0:T(8,128)S(1)}, u32[]{:S(2)}) copy-start(f32[744,768]{1,0:T(8,128)S(1)} %get-tuple-element.443) | copy-start | bytes 6856708
  593.8 7.9 copy-start.16
  608.8 12.6 copy-start.83
  1456.4 9.3 copy-start.8
  1456.4 9.3 copy-start.36
  1465.8 11.0 copy-start.68
  1494.5 8.1 copy-start.23
  1494.5 8.1 copy-start.43
  1512.4 7.3 copy-start.35
  1530.8 9.8 copy-start.20
  1530.9 9.8 copy-start.29
  1540.6 133.6 %reduce-scatter.17.cloned.1.call-start = ((), (), s32[]{:S(2)}) async-start(), calls=%async_computation.18 | async-start | bytes 2654208 | tf_op jit(solution)/shard_map/reduce_scatter | solution.py:282
  1543.2 202.3 %reduce-scatter.11.cloned.1.call-start = ((), (), s32[]{:S(2)}) async-start(), calls=%async_computation.15 | async-start | bytes 2654208 | tf_op jit(solution)/shard_map/reduce_scatter | solution.py:279
  1547.4 270.0 %reduce-scatter.13.cloned.1.call-start = ((), (), s32[]{:S(2)}) async-start(), calls=%async_computation.16 | async-start | bytes 2654208 | tf_op jit(solution)/shard_map/reduce_scatter | solution.py:280
  1551.2 337.8 %reduce-scatter.15.cloned.1.call-start = ((), (), s32[]{:S(2)}) async-start(), calls=%async_computation.17 | async-start | bytes 2654208 | tf_op jit(solution)/shard_map/reduce_scatter | solution.py:281
  1555.1 454.5 %reduce-scatter.19.cloned.1.call-start = ((), (), s32[]{:S(2)}) async-start(), calls=%async_computation.19 | async-start | bytes 7077888 | tf_op jit(solution)/shard_map/reduce_scatter | solution.py:284
  1562.9 567.3 %reduce-scatter.21.cloned.1.call-start = ((), (), s32[]{:S(2)}) async-start(), calls=%async_computation.20 | async-start | bytes 7077888 | tf_op jit(solution)/shard_map/reduce_scatter | solution.py:285
  1569.5 681.2 %reduce-scatter.23.cloned.1.call-start = ((), (), s32[]{:S(2)}) async-start(), calls=%async_computation.21 | async-start | bytes 7077888 | tf_op jit(solution)/shard_map/reduce_scatter | solution.py:286
  1578.0 763.1 %all-reduce.19.cloned.1.call-start = ((), (), s32[]{:S(2)}) async-start(), calls=%async_computation.23 | async-start | bytes 7348224 | tf_op jit(solution)/shard_map/psum | solution.py:288
  2250.8 44.7 %copy-start.77 = (s32[1487]{0:T(1024)S(1)}, s32[1487]{0:T(1024)}, u32[]{:S(2)}) copy-start(s32[1487]{0:T(1024)} %fusion.85) | copy-start | bytes 17848
  2250.8 44.7 %copy-start.87 = (f32[12,1487]{1,0:T(8,128)S(1)}, f32[12,1487]{1,0:T(8,128)}, u32[]{:S(2)}) copy-start(f32[12,1487]{1,0:T(8,128)} %get-tuple-element.214) | copy-start | bytes 214132
  2250.8 45.2 %copy-start.82 = (f32[4]{0:T(128)S(1)}, f32[4]{0:T(128)}, u32[]{:S(2)}) copy-start(f32[4]{0:T(128)} %get-tuple-element.413) | copy-start | bytes 52
  2250.8 83.9 %copy-start.22 = (f32[744,768]{1,0:T(8,128)S(1)}, f32[744,768]{1,0:T(8,128)}, u32[]{:S(2)}) copy-start(f32[744,768]{1,0:T(8,128)} %copy-done.21) | copy-start | bytes 6856708
  2341.1 8.6 copy-start.39
  2341.1 9.4 copy-start.38
  (91 other events, 287.9 us)
Sparse Core Ops, SparseCore 0:
  10.2 44.4 all-gather.8
  56.9 41.2 all-gather.10
  100.3 39.8 all-gather.12
  142.2 39.7 all-gather.14
  184.1 59.2 all-gather.16
  245.4 59.0 all-gather.18
  306.7 59.0 all-gather.20
  1540.7 61.7 reduce-scatter.24
  1606.1 68.0 reduce-scatter.16
  1677.5 68.0 reduce-scatter.10
  1749.1 68.3 reduce-scatter.12
  1820.8 68.2 reduce-scatter.14
  1892.6 116.9 reduce-scatter.18
  2013.0 117.0 reduce-scatter.20
  2133.6 117.1 reduce-scatter.22
  2254.1 78.8 all-reduce.18
where the time goes:
time: 2370 us; the launch traced here: 2360 us
  local copies, waits for them, and re-layouts  1020 us (43%)
  waiting for transfers between devices  673 us (28%)
  matrix products  314 us (13%)
  other arithmetic  195 us (8%)
  blocking collectives  134 us (6%)
    another operation x48, local copies, waits for them, and re-layouts, relative_matrix(): tiled = jnp.tile(vector, length + 1)  246 us
    reshape x24, local copies, waits for them, and re-layouts, relative_matrix(): return flattened.reshape(length, 2 * length - 2)[:, :length]  153 us
    dot_general x43, matrix products, rows_product(): lax.dot_general(left, right, (((1,), (1,)), ((), ())), preferred_element_...  137 us
    reduce_scatter x1, waiting for transfers between devices, body(): lax.psum_scatter(grad_w_gate, 'wide', scatter_dimension=0, tiled=True)  121 us
    reduce_scatter x1, waiting for transfers between devices, body(): lax.psum_scatter(grad_w_up, 'wide', scatter_dimension=0, tiled=True)  121 us
    reduce_scatter x1, waiting for transfers between devices, body(): lax.psum_scatter(grad_down, 'wide', scatter_dimension=0, tiled=True)  121 us
    slice x24, local copies, waits for them, and re-layouts, relative_matrix(): lax.slice(tiled, (length - 1,), (length - 1 + length * (2 * length - 2),))  104 us
    reshape x12, local copies, waits for them, and re-layouts, diagonal_totals(): return jnp.sum(flattened.reshape(length + 1, 2 * length - 1), axis=0)  92.1 us
  transfers between devices with their start and end apart: 16, of which 8 were waited for; matrix products, arithmetic and copies ran while one was open for 24% of the time, Pallas kernels for 0%

commit v1 on v0

v1 whole, which is shorter than its diff:
```python
import functools

import jax
import jax.numpy as jnp
from jax import lax
from jax.experimental import pallas as pl
from jax.experimental.pallas import tpu as pltpu
from jax.sharding import PartitionSpec as P

f32 = jnp.float32
bf16 = jnp.bfloat16
TP = 768
BLK = 128
NB = TP // BLK
LEFT = TP - BLK
STRIP = 2 * TP - BLK
W0 = LEFT - 128
WN = 384

def nt(a, b):
    return lax.dot_general(a, b, (((1,), (1,)), ((), ())), preferred_element_type=f32)

def nn(a, b):
    return lax.dot_general(a, b, (((1,), (0,)), ((), ())), preferred_element_type=f32)

def build_masks(scal_ref, kaug, raug, ntok):
    joined = scal_ref[0] == 1
    l0 = scal_ref[1]; l1 = scal_ref[2]
    half = ntok // 2
    u = lax.broadcasted_iota(jnp.int32, (TP, 128), 0)
    lane = lax.broadcasted_iota(jnp.int32, (TP, 128), 1)
    seg = (u >= half).astype(jnp.int32)
    lim = jnp.where(seg == 1, l1, l0)
    start = seg * half
    lim = jnp.where(joined, l0 + l1, lim)
    start = jnp.where(joined, 0, start)
    valid = (2 * (u - start) < lim) & (u < ntok)
    segs = jnp.where(joined, 0, seg)
    ok = valid & (segs == lane)
    kaug[...] = jnp.where((lane < 2) & jnp.logical_not(ok), -1e30, 0.0).astype(bf16)
    t = u
    rows = jnp.where((lane == segs), 1.0, 0.0).astype(bf16)
    for b in range(NB):
        blk = rows[b * 128:(b + 1) * 128]
        raug[b] = jnp.concatenate([blk, blk], axis=0)

def build_strip(base_ref, row0, strip):
    for hh in range(2):
        row = base_ref[pl.ds(row0 + hh, 1), :]
        cl = row[:, 0:1]; cr = row[:, 383:384]
        sq = jnp.broadcast_to(row, (128, 512))
        sq = pltpu.roll(sq, 0, 1, stride=1, stride_axis=0)
        win = sq[:, :WN].T
        lanes = slice(hh * 128, hh * 128 + 128)
        strip[0:W0, lanes] = jnp.broadcast_to(cl, (W0, 128))
        strip[W0:W0 + WN, lanes] = win
        strip[W0 + WN:STRIP, lanes] = jnp.broadcast_to(cr, (STRIP - W0 - WN, 128))

def stacked(blk):
    lane = lax.broadcasted_iota(jnp.int32, blk.shape, 1)
    z = jnp.zeros_like(blk)
    return jnp.concatenate([jnp.where(lane < 64, blk, z), jnp.where(lane >= 64, blk, z)], axis=0)

def fwd_kernel(ntok, scal_ref, q_ref, k_ref, v_ref, base_ref, o_ref, lse_ref, kaug, raug, strip, vt):
    p = pl.program_id(0)
    @pl.when(p == 0)
    def _():
        build_masks(scal_ref, kaug, raug, ntok)
    build_strip(base_ref, 2 * p, strip)
    vt[...] = v_ref[...].T
    kcat = jnp.concatenate([k_ref[...], kaug[...]], axis=1)
    vtv = vt[...]
    rowsel = lax.broadcasted_iota(jnp.int32, (128, 128), 0) < 64
    for b in range(NB):
        rhs = jnp.concatenate([stacked(q_ref[b * 128:(b + 1) * 128, :]), raug[b]], axis=1)
        s = nt(kcat, rhs) + strip[LEFT - b * 128:LEFT - b * 128 + TP, :]
        mx = jnp.max(s, axis=0, keepdims=True)
        e = jnp.exp(s - mx)
        l = jnp.sum(e, axis=0, keepdims=True)
        ot = nn(vtv, e.astype(bf16)) * (1.0 / l)
        lse_ref[0, b:b + 1, :] = mx + jnp.log(l)
        o = jnp.where(rowsel, ot[:, :128], ot[:, 128:])
        o_ref[b * 128:(b + 1) * 128, :] = o.T.astype(bf16)

def attn_forward(scal, q, k, v, base2, ntok):
    heads = base2.shape[0]
    pairs = heads // 2
    col = pl.BlockSpec((TP, 128), lambda p: (0, p))
    return pl.pallas_call(
        functools.partial(fwd_kernel, ntok),
        grid=(pairs,),
        out_shape=(jax.ShapeDtypeStruct((TP, heads * 64), bf16), jax.ShapeDtypeStruct((pairs, 8, 256), f32)),
        in_specs=[pl.BlockSpec(memory_space=pltpu.SMEM), col, col, col, pl.BlockSpec(memory_space=pltpu.VMEM)],
        out_specs=(col, pl.BlockSpec((1, 8, 256), lambda p: (p, 0, 0))),
        scratch_shapes=[pltpu.VMEM((TP, 128), bf16), pltpu.VMEM((NB, 256, 128), bf16), pltpu.VMEM((STRIP, 256), f32), pltpu.VMEM((128, TP), bf16)],
        compiler_params=pltpu.CompilerParams(vmem_limit_bytes=48 << 20),
        name="attn_fwd",
    )(scal, q, k, v, base2)

def bwd_kernel(ntok, scal_ref, q_ref, k_ref, v_ref, g_ref, lse_ref, base_ref, dq_ref, dk_ref, dv_ref, db_ref, kaug, raug, strip, acc, kt, dk_s, dv_s):
    p = pl.program_id(0)
    @pl.when(p == 0)
    def _():
        build_masks(scal_ref, kaug, raug, ntok)
    build_strip(base_ref, 2 * p, strip)
    kt[...] = k_ref[...].T
    kcat = jnp.concatenate([k_ref[...], kaug[...]], axis=1)
    v = v_ref[...]
    ktv = kt[...]
    acc[...] = jnp.zeros_like(acc)
    dk_s[...] = jnp.zeros_like(dk_s)
    dv_s[...] = jnp.zeros_like(dv_s)
    rowsel = lax.broadcasted_iota(jnp.int32, (128, 128), 0) < 64
    for b in range(NB):
        qs = stacked(q_ref[b * 128:(b + 1) * 128, :])
        gs = stacked(g_ref[b * 128:(b + 1) * 128, :])
        rhs = jnp.concatenate([qs, raug[b]], axis=1)
        w = slice(LEFT - b * 128, LEFT - b * 128 + TP)
        s = nt(kcat, rhs) + strip[w, :]
        pr = jnp.exp(s - lse_ref[0, b:b + 1, :])
        dp = nt(v, gs)
        pdp = pr * dp
        delta = jnp.sum(pdp, axis=0, keepdims=True)
        ds = pdp - pr * delta
        acc[w, :] += ds
        dsb = ds.astype(bf16)
        dk_s[...] += nn(dsb, qs)
        dv_s[...] += nn(pr.astype(bf16), gs)
        dqt = nn(ktv, dsb)
        dq = jnp.where(rowsel, dqt[:, :128], dqt[:, 128:])
        dq_ref[b * 128:(b + 1) * 128, :] = dq.T.astype(bf16)
    dk_ref[...] = dk_s[...].astype(bf16)
    dv_ref[...] = dv_s[...].astype(bf16)
    fi = lax.broadcasted_iota(jnp.int32, (128, 128), 0)
    fj = lax.broadcasted_iota(jnp.int32, (128, 128), 1)
    flip = jnp.where(fi + fj == 127, 1.0, 0.0).astype(f32)
    for hh in range(2):
        lanes = slice(hh * 128, hh * 128 + 128)
        far_l = jnp.sum(acc[0:W0, lanes], keepdims=True)
        far_r = jnp.sum(acc[W0 + WN:STRIP, lanes], keepdims=True)
        win = acc[W0:W0 + WN, lanes]
        wt = lax.dot_general(flip, win, (((1,), (1,)), ((), ())), precision=lax.Precision.HIGHEST, preferred_element_type=f32)
        wt = jnp.concatenate([wt, jnp.zeros((128, 128), f32)], axis=1)
        wt = pltpu.roll(wt, 0, 1, stride=1, stride_axis=0)
        diag = jnp.sum(wt, axis=0, keepdims=True)
        lane = lax.broadcasted_iota(jnp.int32, (1, 512), 1)
        diag = diag + jnp.where(lane == 0, far_l, 0.0) + jnp.where(lane == 510, far_r, 0.0)
        db_ref[0, hh:hh + 1, :] = diag

def attn_backward(scal, q, k, v, g, lse, base2, ntok):
    heads = base2.shape[0]
    pairs = heads // 2
    col = pl.BlockSpec((TP, 128), lambda p: (0, p))
    sd = jax.ShapeDtypeStruct((TP, heads * 64), bf16)
    return pl.pallas_call(
        functools.partial(bwd_kernel, ntok),
        grid=(pairs,),
        out_shape=(sd, sd, sd, jax.ShapeDtypeStruct((pairs, 8, 512), f32)),
        in_specs=[pl.BlockSpec(memory_space=pltpu.SMEM), col, col, col, col, pl.BlockSpec((1, 8, 256), lambda p: (p, 0, 0)), pl.BlockSpec(memory_space=pltpu.VMEM)],
        out_specs=(col, col, col, pl.BlockSpec((1, 8, 512), lambda p: (p, 0, 0))),
        scratch_shapes=[pltpu.VMEM((TP, 128), bf16), pltpu.VMEM((NB, 256, 128), bf16), pltpu.VMEM((STRIP, 256), f32), pltpu.VMEM((STRIP, 256), f32), pltpu.VMEM((128, TP), bf16),
                        pltpu.VMEM((TP, 128), f32), pltpu.VMEM((TP, 128), f32)],
        compiler_params=pltpu.CompilerParams(vmem_limit_bytes=48 << 20),
        name="attn_bwd",
    )(scal, q, k, v, g, lse, base2)

def bucket_of(relative):
    distance = jnp.abs(relative)
    far = 8 + sum(((distance >= e).astype(jnp.int32) for e in (12, 16, 23, 32, 46, 64, 91)))
    near = jnp.where(distance < 8, distance, far)
    return near + 16 * (relative > 0).astype(jnp.int32)

def base_hot(nbuckets, grad=False):
    c = jnp.arange(512, dtype=jnp.int32)
    r = c - 255 if grad else jnp.where(c < 384, c - 128, c - 640)
    return (bucket_of(r)[:, None] == jnp.arange(nbuckets, dtype=jnp.int32)[None, :]).astype(f32)


ROWS = 128
VP = 384
VR = 272
EPS = 1e-6

def byte_valid_mat(scal_ref, nbytes):
    i = lax.broadcasted_iota(jnp.int32, (ROWS, 128), 0)
    j = lax.broadcasted_iota(jnp.int32, (ROWS, 128), 1)
    p = 12 * i + j
    slot = nbytes // 2
    joined = scal_ref[0] == 1
    l0 = scal_ref[1]; l1 = scal_ref[2]
    second = p >= slot
    start = jnp.where(joined, 0, jnp.where(second, slot, 0))
    lim = jnp.where(joined, l0 + l1, jnp.where(second, l1, l0))
    ok = (p - start < lim) & (p < nbytes) & (j < 12)
    return jnp.where(ok, 1.0, 0.0).astype(f32)

def inverse_counts(vm):
    v = [vm[:, j:j + 1] for j in range(12)]
    inv = {1: v}
    for b in (2, 3, 4):
        out = []
        for m in range(12 // b):
            tot = v[b * m]
            for t in range(1, b):
                tot = tot + v[b * m + t]
            out.append(1.0 / jnp.maximum(tot, 1.0))
        inv[b] = out
    return v, inv

def softmax_weights(e, inv):
    rate = {1: e}
    for b in (2, 3, 4):
        out = []
        for m in range(12 // b):
            tot = e[b * m]
            for t in range(1, b):
                tot = tot + e[b * m + t]
            out.append(tot * inv[b][m])
        rate[b] = out
    w = {b: [] for b in (1, 2, 3, 4)}
    for p in range(12):
        r = [rate[b][p // b] for b in (1, 2, 3, 4)]
        mx = jnp.maximum(jnp.maximum(r[0], r[1]), jnp.maximum(r[2], r[3]))
        ex = [jnp.exp(x - mx) for x in r]
        inv_t = 1.0 / (ex[0] + ex[1] + ex[2] + ex[3])
        for b in (1, 2, 3, 4):
            w[b].append(ex[b - 1] * inv_t)
    return w

def gbst_fwd_body(nbytes, scal_ref, ids_ref, table_ref, score_ref, gain_ref, stream_ref, normed_ref, emb_ref, wcol_ref, tot_ref, slabs):
    vm = byte_valid_mat(scal_ref, nbytes)
    v, inv = inverse_counts(vm)
    idt = ids_ref[...].astype(f32).T
    lane = lax.broadcasted_iota(jnp.int32, (ROWS, VP), 1).astype(f32)
    s = score_ref[...].astype(f32)
    e = []
    for j in range(12):
        hot = jnp.where((lane == idt[:, j:j + 1]) & (v[j] > 0.5), 1.0, 0.0).astype(bf16)
        ej = nn(hot, table_ref[...])
        emb_ref[j * ROWS:(j + 1) * ROWS, :] = ej.astype(bf16)
        e.append(jnp.sum(ej * s, axis=1, keepdims=True))
    w = softmax_weights(e, inv)
    l128 = lax.broadcasted_iota(jnp.int32, (ROWS, 128), 1)
    wc = jnp.zeros((ROWS, 128), f32)
    for b in (1, 2, 3, 4):
        for p in range(12):
            wc = jnp.where(l128 == (b - 1) * 12 + p, w[b][p], wc)
    wcol_ref[...] = wc
    tl = lax.broadcasted_iota(jnp.int32, (8, 128), 1)
    tot = jnp.zeros((8, 128), f32)
    for b in (1, 2, 3, 4):
        acc = w[b][0] * v[0]
        for p in range(1, 12):
            acc = acc + w[b][p] * v[p]
        tot = jnp.where(tl == b - 1, jnp.sum(acc, keepdims=True), tot)
    tot = jnp.where(tl == 4, jnp.sum(vm, keepdims=True), tot)
    tot_ref[...] = tot
    E = lambda j: emb_ref[j * ROWS:(j + 1) * ROWS, :].astype(f32)
    for k in range(6):
        p0, p1 = 2 * k, 2 * k + 1
        b2 = 0.5 * (w[2][p0] + w[2][p1]) * inv[2][k]
        acc = (0.5 * w[1][p0] + b2) * E(p0) + (0.5 * w[1][p1] + b2) * E(p1)
        n = k // 2
        d = 0.5 * (w[4][p0] + w[4][p1]) * inv[4][n]
        acc = acc + d * ((E(4 * n) + E(4 * n + 1)) + (E(4 * n + 2) + E(4 * n + 3)))
        m0, m1 = p0 // 3, p1 // 3
        s3 = lambda m: E(3 * m) + E(3 * m + 1) + E(3 * m + 2)
        if m0 == m1:
            acc = acc + (0.5 * (w[3][p0] + w[3][p1]) * inv[3][m0]) * s3(m0)
        else:
            acc = acc + (0.5 * w[3][p0] * inv[3][m0]) * s3(m0) + (0.5 * w[3][p1] * inv[3][m1]) * s3(m1)
        put_strided(slabs, k, acc)
    ntok = nbytes // 2
    for c in range(slabs.shape[0]):
        stream_ref[0:ntok, c * 128:(c + 1) * 128] = slabs[c, 0:ntok, :]
    stream_ref[ntok:TP, :] = jnp.zeros((TP - ntok, acc.shape[1]), f32)
    norm_rows(stream_ref, gain_ref, normed_ref)

def put_strided(ref, k, val):
    for c in range(val.shape[1] // 128):
        ref[c, pl.ds(k, 124, stride=6), :] = val[:124, c * 128:(c + 1) * 128]

def get_strided(ref, k):
    parts = [ref[c, pl.ds(k, 124, stride=6), :] for c in range(ref.shape[0])]
    x = jnp.concatenate(parts, axis=1)
    return jnp.concatenate([x, jnp.zeros((4, x.shape[1]), f32)], axis=0)

def norm_rows(x_ref, gain_ref, out_ref):
    g = gain_ref[...].astype(f32)
    for b in range(TP // 128):
        x = x_ref[b * 128:(b + 1) * 128, :]
        sc = lax.rsqrt(jnp.mean(x * x, axis=1, keepdims=True) + EPS)
        out_ref[b * 128:(b + 1) * 128, :] = (x * sc * g).astype(bf16)

def gbst_bwd_body(nbytes, scal_ref, ids_ref, emb_ref, wcol_ref, score_ref, gs_ref, gtable_ref, gscore_ref, de_ref, slabs):
    for c in range(slabs.shape[0]):
        slabs[c] = gs_ref[:, c * 128:(c + 1) * 128]
    vm = byte_valid_mat(scal_ref, nbytes)
    v, inv = inverse_counts(vm)
    wc = wcol_ref[...]
    w = {b: [wc[:, (b - 1) * 12 + p:(b - 1) * 12 + p + 1] for p in range(12)] for b in (1, 2, 3, 4)}
    s = score_ref[...].astype(f32)
    E = lambda j: emb_ref[j * ROWS:(j + 1) * ROWS, :].astype(f32)
    s3 = lambda m: E(3 * m) + E(3 * m + 1) + E(3 * m + 2)
    s4 = lambda n: (E(4 * n) + E(4 * n + 1)) + (E(4 * n + 2) + E(4 * n + 3))
    dot = lambda a, b: jnp.sum(a * b, axis=1, keepdims=True)
    dw = {b: [None] * 12 for b in (1, 2, 3, 4)}
    D = []
    for k in range(6):
        dk = 0.5 * get_strided(slabs, k)
        D.append(dk)
        p0, p1 = 2 * k, 2 * k + 1
        x0, x1 = dot(dk, E(p0)), dot(dk, E(p1))
        dw[1][p0], dw[1][p1] = x0, x1
        dw[2][p0] = dw[2][p1] = (x0 + x1) * inv[2][k]
        m0, m1 = p0 // 3, p1 // 3
        a0 = dot(dk, s3(m0)) * inv[3][m0]
        dw[3][p0] = a0
        dw[3][p1] = a0 if m0 == m1 else dot(dk, s3(m1)) * inv[3][m1]
        dw[4][p0] = dw[4][p1] = dot(dk, s4(k // 2)) * inv[4][k // 2]
    dr = {b: [] for b in (1, 2, 3, 4)}
    for p in range(12):
        mean = w[1][p] * dw[1][p] + w[2][p] * dw[2][p] + w[3][p] * dw[3][p] + w[4][p] * dw[4][p]
        for b in (1, 2, 3, 4):
            dr[b].append(w[b][p] * (dw[b][p] - mean))
    rb = {1: dr[1]}
    for b in (2, 3, 4):
        out = []
        for m in range(12 // b):
            tot = dr[b][b * m]
            for t in range(1, b):
                tot = tot + dr[b][b * m + t]
            out.append(tot * inv[b][m])
        rb[b] = out
    t3 = []
    for m in range(4):
        terms = {}
        for p in (3 * m, 3 * m + 1, 3 * m + 2):
            terms[p // 2] = terms[p // 2] + w[3][p] if p // 2 in terms else w[3][p]
        acc = None
        for k, coef in terms.items():
            t = (coef * inv[3][m]) * D[k]
            acc = t if acc is None else acc + t
        t3.append(acc)
    gscore = jnp.zeros((8, s.shape[1]), f32)
    for n in range(3):
        t4 = ((w[4][4 * n] + w[4][4 * n + 1]) * inv[4][n]) * D[2 * n] + ((w[4][4 * n + 2] + w[4][4 * n + 3]) * inv[4][n]) * D[2 * n + 1]
        for p in range(4 * n, 4 * n + 4):
            k = p // 2
            c = rb[1][p] + rb[2][k] + rb[3][p // 3] + rb[4][n]
            b2 = (w[2][2 * k] + w[2][2 * k + 1]) * inv[2][k]
            de = v[p] * ((w[1][p] + b2) * D[k] + t3[p // 3] + t4 + c * s)
            de_ref[p * ROWS:(p + 1) * ROWS, :] = de.astype(bf16)
            y = c * E(p)
            gscore = gscore + jnp.sum(y.reshape(ROWS // 8, 8, s.shape[1]), axis=0)
    gscore_ref[...] = jnp.sum(gscore, axis=0, keepdims=True)
    row = lax.broadcasted_iota(jnp.int32, (VR, ROWS), 0)
    hots = [jnp.where(row == ids_ref[j:j + 1, :], 1.0, 0.0).astype(bf16) for j in range(12)]
    hot = jnp.concatenate(hots, axis=1)
    gtable_ref[...] = nn(hot, de_ref[...])

def gbst_forward(scal, ids, table, score, gain, nbytes):
    d = table.shape[1]
    vm = pl.BlockSpec(memory_space=pltpu.VMEM)
    return pl.pallas_call(
        functools.partial(gbst_fwd_body, nbytes),
        out_shape=(jax.ShapeDtypeStruct((TP, d), f32), jax.ShapeDtypeStruct((TP, d), bf16), jax.ShapeDtypeStruct((12 * ROWS, d), bf16),
                   jax.ShapeDtypeStruct((ROWS, 128), f32), jax.ShapeDtypeStruct((8, 128), f32)),
        in_specs=[pl.BlockSpec(memory_space=pltpu.SMEM)] + [vm] * 4,
        out_specs=(vm,) * 5,
        scratch_shapes=[pltpu.VMEM((d // 128, TP, 128), f32)],
        compiler_params=pltpu.CompilerParams(vmem_limit_bytes=48 << 20),
        name="gbst_fwd",
    )(scal, ids, table, score, gain)

def gbst_backward(scal, ids, emb, wcol, score, gs, nbytes):
    d = emb.shape[1]
    vm = pl.BlockSpec(memory_space=pltpu.VMEM)
    return pl.pallas_call(
        functools.partial(gbst_bwd_body, nbytes),
        out_shape=(jax.ShapeDtypeStruct((VR, d), f32), jax.ShapeDtypeStruct((1, d), f32)),
        in_specs=[pl.BlockSpec(memory_space=pltpu.SMEM)] + [vm] * 5,
        out_specs=(vm, vm),
        scratch_shapes=[pltpu.VMEM((12 * ROWS, d), bf16), pltpu.VMEM((d // 128, TP, 128), f32)],
        compiler_params=pltpu.CompilerParams(vmem_limit_bytes=48 << 20),
        name="gbst_bwd",
    )(scal, ids, emb, wcol, score, gs)


def tn(a, b):
    return lax.dot_general(a, b, (((0,), (0,)), ((), ())), preferred_element_type=f32)


def norm_back(x, gain, gy):
    s = lax.rsqrt(jnp.mean(x * x, axis=1, keepdims=True) + EPS)
    t = gy * gain
    gx = s * t - x * (s * s * s) * jnp.mean(x * t, axis=1, keepdims=True)
    return gx, jnp.sum(gy * x * s, axis=0)


def layer(byte_ids, lengths, bucket, out_grad, table, score, gain_one, wq, wk, wv, wo, rel_bias, gain_two, wg, wu, wd):
    ids = byte_ids[0]
    nbytes = ids.shape[0]
    ntok = nbytes // 2
    d = table.shape[1]
    vocab = table.shape[0]
    scal = jnp.stack([bucket[0], lengths[0, 0], lengths[0, 1]])
    idp = jnp.pad(ids.reshape(nbytes // 12, 12).T, ((0, 4), (0, ROWS - nbytes // 12)), constant_values=-1)
    tp = jnp.pad(table, ((0, VP - vocab), (0, 0)))
    stream, normed, emb, wcol, tot = gbst_forward(scal, idp, tp, score[None], gain_one[None], nbytes)
    q = nn(normed, wq).astype(bf16)
    k = nn(normed, wk).astype(bf16)
    v = nn(normed, wv).astype(bf16)
    nb = rel_bias.shape[0]
    base2 = jnp.dot(base_hot(nb), rel_bias.astype(f32), precision=lax.Precision.HIGHEST).T
    mixed, lse = attn_forward(scal, q, k, v, base2, ntok)
    middle = stream + nn(mixed, wo)
    g2 = gain_two.astype(f32)
    s2 = lax.rsqrt(jnp.mean(middle * middle, axis=1, keepdims=True) + EPS)
    normed_ff = (middle * s2 * g2).astype(bf16)
    gate = nn(normed_ff, wg)
    up = nn(normed_ff, wu)
    c0 = 0.7978845608028654
    inner = c0 * (gate + 0.044715 * gate * gate * gate)
    th = jnp.tanh(inner)
    act = 0.5 * gate * (1.0 + th)
    hidden = (act * up).astype(bf16)
    encoded = (middle + nn(hidden, wd)).astype(bf16)[:ntok][None]
    og = jnp.pad(out_grad[0], ((0, TP - ntok), (0, 0)))
    g_wd = tn(hidden, og)
    gh = nt(og, wd)
    dact = 0.5 * (1.0 + th) + 0.5 * gate * (1.0 - th * th) * (c0 * (1.0 + 3 * 0.044715 * gate * gate))
    gg = (gh * up * dact).astype(bf16)
    gu = (gh * act).astype(bf16)
    g_wg = tn(normed_ff, gg)
    g_wu = tn(normed_ff, gu)
    g_nff = nt(gg, wg) + nt(gu, wu)
    gx2, g_gain2 = norm_back(middle, g2, g_nff)
    g_mid = og.astype(f32) + gx2
    g_br = g_mid.astype(bf16)
    g_wo = tn(mixed, g_br)
    g_heads = nt(g_br, wo).astype(bf16)
    dq, dk, dv, db = attn_backward(scal, q, k, v, g_heads, lse, base2, ntok)
    g_rel = jnp.dot(base_hot(nb, True).T, db[:, :2, :].reshape(rel_bias.shape[1], 512).T, precision=lax.Precision.HIGHEST)
    g_wq = tn(normed, dq)
    g_wk = tn(normed, dk)
    g_wv = tn(normed, dv)
    g_n = nt(dq, wq) + nt(dk, wk) + nt(dv, wv)
    gx1, g_gain1 = norm_back(stream, gain_one.astype(f32), g_n)
    g_stream = g_mid + gx1
    g_table, g_score = gbst_backward(scal, idp, emb, wcol, score[None], g_stream, nbytes)
    return encoded, g_table[:vocab], g_score[0], g_gain1, g_wq, g_wk, g_wv, g_wo, g_rel, g_gain2, g_wg, g_wu, g_wd, tot[0, :5]


def body(byte_ids, lengths, bucket, out_grad, *weights):
    axes = (1, 0, 0, 0, 0, 0, 0, None, 0, 0, 0, 0)
    full = [w if a is None else lax.all_gather(w, "wide", axis=a, tiled=True) for w, a in zip(weights, axes)]
    out = layer(byte_ids, lengths, bucket, out_grad, *full)
    encoded, grads, tot = out[0], out[1:13], out[13]
    final = [None] * 12
    grads = list(grads)
    scatter = {0: 1, 3: 0, 4: 0, 5: 0, 6: 0, 9: 0, 10: 0, 11: 0}
    for i, dim in scatter.items():
        part = lax.psum_scatter(grads[i].astype(bf16), "wide", scatter_dimension=dim, tiled=True)
        final[i] = lax.psum(part, "narrow").astype(f32)
    rel, score, gain1, gain2, tot = lax.psum((grads[7], grads[1], grads[2], grads[8], tot), ("wide", "narrow"))
    w = lax.axis_index("wide")
    n = weights[1].shape[0]
    cut = lambda x: lax.dynamic_slice(x, (w * n,), (n,))
    final[1], final[2], final[7], final[8] = cut(score), cut(gain1), rel, cut(gain2)
    return (encoded, *final, tot[:4] / tot[4])


def solution(mesh):
    both = ("wide", "narrow")
    rows = P("wide", None)
    vec = P("wide")
    placed = (P(both, None), P(both, None), P(both), P(both, None, None), P(None, "wide"), vec, vec, rows, rows, rows, rows, P(), vec, rows, rows, rows)
    outs = (P(both, None, None), P(None, "wide"), vec, vec, rows, rows, rows, rows, P(), vec, rows, rows, rows, P())
    return jax.shard_map(body, mesh=mesh, in_specs=placed, out_specs=outs, check_vma=False)
```

time: 2370 us -> 1060 us (0.45)
  local copies, waits for them, and re-layouts: 1020 us -> 25.9 us
  matrix products: 314 us -> 92.9 us
  other arithmetic: 195 us -> 17.8 us
  Pallas kernels: 0 us -> 72 us
  waiting for transfers between devices: 673 us -> 720 us
  blocking collectives: 134 us -> 107 us
    reshape x63 -> x1, local copies, waits for them, and re-layouts: 386 us -> 0.02 us  [layer(): db[:, :2, :].reshape(rel_bias.shape[1], 512)]
    reduce_scatter x7, waiting for transfers between devices: 647 us -> 394 us  [body(): lax.psum_scatter(grads[i].astype(bf16), 'wide', scatter_dimension=dim, ti...]
    another operation x56 -> x2, local copies, waits for them, and re-layouts: 252 us -> 0.17 us  [layer(): ids.reshape(nbytes // 12, 12)]
    all_gather x7, waiting for transfers between devices: 0.05 us -> 227 us  [body(): lax.all_gather(w, 'wide', axis=a, tiled=True)]
    dot_general x108 -> x23, matrix products: 304 us -> 92.9 us  [the longest x7 33.4 us: tn(): lax.dot_general(a, b, (((0,), (0,)), ((), ())), preferred_element_type=f32)]
    slice x75 -> x4, local copies, waits for them, and re-layouts: 145 us -> 2.11 us  [the longest x1 0.9 us: layer(): db[:, :2, :].reshape(rel_bias.shape[1], 512)]
    reduce_sum x51 -> x1, other arithmetic: 124 us -> 0.22 us  [norm_back(): s = lax.rsqrt(jnp.mean(x * x, axis=1, keepdims=True) + EPS)]
    pallas_call x0 -> x4, Pallas kernels: none -> 72 us  [the longest x1 31.3 us: attn_backward(): pl.pallas_call(functools.partial(bwd_kernel, ntok), grid=(pairs,), out_sh...]
  transfers between devices with their start and end apart: 16 -> 16, of which waited for: 8 -> 14; matrix products, arithmetic and copies ran while one was open for 24% -> 9% of each run, Pallas kernels for 0% -> 4%
where the time goes in v1:
time: 1060 us; the launch traced here: 1050 us
  waiting for transfers between devices  720 us (68%)
  blocking collectives  107 us (10%)
  matrix products  92.9 us (9%)
  Pallas kernels  72 us (7%)
  local copies, waits for them, and re-layouts  25.9 us (2%)
  other arithmetic  17.8 us (2%)
  between operations  16.3 us (2%)
    reduce_scatter x7, waiting for transfers between devices, body(): lax.psum_scatter(grads[i].astype(bf16), 'wide', scatter_dimension=dim, ti...  394 us
    all_gather x7, waiting for transfers between devices, body(): lax.all_gather(w, 'wide', axis=a, tiled=True)  227 us
    unnamed x17, waiting for transfers between devices  62.6 us
    psum x1, blocking collectives, body(): lax.psum((grads[7], grads[1], grads[2], grads[8], tot), ('wide', 'narrow'))  40 us
    psum x1, waiting for transfers between devices, body(): final[i] = lax.psum(part, 'narrow').astype(f32)  36 us
    dot_general x7, matrix products, tn(): lax.dot_general(a, b, (((0,), (0,)), ((), ())), preferred_element_type=f32)  33.4 us
    dot_general x7, matrix products, nn(): lax.dot_general(a, b, (((1,), (0,)), ((), ())), preferred_element_type=f32)  32.7 us
    all_gather x1, blocking collectives, body(): lax.all_gather(w, 'wide', axis=a, tiled=True)  31.8 us
  transfers between devices with their start and end apart: 16, of which 14 were waited for; matrix products, arithmetic and copies ran while one was open for 9% of the time, Pallas kernels for 4%

profile of v1, /device:TPU:0, one launch (start us, length us, event | category | flops | bytes accessed | tf_op | source)
XLA Modules:
  0.0 1052.3 jit_solution(10976980771315828475)
XLA Ops:
  12.0 1.2 dynamic-slice
  16.4 23.4 %all-reduce.7 = (bf16[768]{0:T(1024)(128)(2,1)S(1)}, bf16[768]{0:T(1024)(128)(2,1)S(1)}, bf16[768]{0:T(1024)(128)(2,1)S(1)}) all-reduce(bf16[768]{0:T(1024)(128)(2,1)S(1)} %dynamic-update-slice, bf16[768]{0:T(1024)(128)(2,1)S(1)} %dynamic-update-slice.1, ...), channel_id=1, replica_groups=mesh['wide'=8,'narrow'=4] {'wide'}, use_global_device_ids=true, to_apply=%add.3 | all-reduce | flops 2304 | bytes 9216
  41.4 31.8 %all-gather = bf16[8,96,259]{1,2,0:T(8,128)(2,1)S(1)} all-gather(bf16[1,96,259]{1,2,0:T(8,128)(2,1)} %bitcast.66), channel_id=1, replica_groups=mesh['wide'=8,'narrow'=4] {'wide'}, dimensions={0}, use_global_device_ids=true | all-gather | bytes 447552 | tf_op jit(solution)/shard_map/all_gather | solution.py:457
  75.0 1.4 pad_add_fusion.scal_ref
  76.4 9.2 gbst_fwd.1
  88.8 2.7 convolution_convert_fusion.10.q_ref
  91.5 8.6 all-gather.13.cloned.1.call-done
  100.2 3.7 convolution_convert_fusion.8.v_ref
  103.9 38.3 %all-gather.11.cloned.1.call-done = bf16[768,768]{1,0:T(8,128)(2,1)} async-done(((bf16[96,768]{1,0:T(8,128)(2,1)}), bf16[768,768]{1,0:T(8,128)(2,1)}) %all-gather.11.cloned.1.call-update) | async-done | bytes 1179664 | tf_op jit(solution)/shard_map/all_gather | solution.py:457
  142.2 2.8 convolution_convert_fusion.9.k_ref
  145.0 19.8 %attn_fwd.1 = (bf16[768,768]{1,0:T(8,128)(2,1)S(1)}, f32[6,8,256]{2,1,0:T(8,128)S(1)}) custom-call(s32[3]{0:T(128)S(1)} %copy-done.16, bf16[768,768]{1,0:T(8,128)(2,1)S(1)} %convolution_convert_fusion.10.q_ref, bf16[768,768]{1,0:T(8,128)(2,1)S(1)} %convolution_convert_fusion.9.k_ref, bf16[768,768]{1,0:T(8,128)(2,1)S(1)} %copy-done.2, f32[12,512]{1,0:T(8,128)S(1)} %copy-done.9), custom_call_target="tpu_custom_call" | custom-call | tf_op jit(solution)/shard_map/attn_fwd/pallas_call | solution.py:89
  167.5 16.6 %all-gather.15.cloned.1.call-done = bf16[768,768]{1,0:T(8,128)(2,1)} async-done(((bf16[96,768]{1,0:T(8,128)(2,1)}), bf16[768,768]{1,0:T(8,128)(2,1)}) %all-gather.15.cloned.1.call-update) | async-done | bytes 1179664 | tf_op jit(solution)/shard_map/all_gather | solution.py:457
  184.1 2.8 multiply_reduce_fusion.5
  188.3 1.3 multiply_convert_fusion.2
  189.6 55.8 %all-gather.17.cloned.1.call-done = bf16[768,2048]{1,0:T(8,128)(2,1)} async-done(((bf16[96,2048]{1,0:T(8,128)(2,1)}), bf16[768,2048]{1,0:T(8,128)(2,1)}) %all-gather.17.cloned.1.call-update) | async-done | bytes 3145744 | tf_op jit(solution)/shard_map/all_gather | solution.py:457
  245.4 7.5 fusion.35
  252.9 53.6 %all-gather.19.cloned.1.call-done = bf16[768,2048]{1,0:T(8,128)(2,1)} async-done(((bf16[96,2048]{1,0:T(8,128)(2,1)}), bf16[768,2048]{1,0:T(8,128)(2,1)}) %all-gather.19.cloned.1.call-update) | async-done | bytes 3145744 | tf_op jit(solution)/shard_map/all_gather | solution.py:457
  306.5 7.5 fusion.36
  314.1 53.7 %all-gather.21.cloned.1.call-done = bf16[2048,768]{1,0:T(8,128)(2,1)} async-done(((bf16[256,768]{1,0:T(8,128)(2,1)}), bf16[2048,768]{1,0:T(8,128)(2,1)}) %all-gather.21.cloned.1.call-update) | async-done | bytes 3145744 | tf_op jit(solution)/shard_map/all_gather | solution.py:457
  367.8 12.9 %multiply_convert_fusion = (bf16[768,2048]{1,0:T(8,128)(2,1)S(1)}, bf16[768,2048]{1,0:T(8,128)(2,1)S(1)}, bf16[768,2048]{1,0:T(8,128)(2,1)}) fusion(f32[768,2048]{1,0:T(8,128)} %fusion.35, f32[768,2048]{1,0:T(8,128)} %fusion.36, bf16[2048,768]{1,0:T(8,128)(2,1)} %all-gather.21.cloned.1.call-done, bf16[744,768]{1,0:T(8,128)(2,1)} %bitcast.62), kind=kOutput, calls=%fused_computation.10 | convolution fusion | flops 2455240704 | bytes 26308608 | tf_op jit(solution)/shard_map/dot_general | solution.py:21
  380.8 2.7 fusion.38
  384.2 1.5 copy-done.48
  385.6 3.5 multiply_reduce_fusion
  390.5 2.2 convolution_convert_fusion.7.g_ref
  392.6 31.3 %attn_bwd.1 = (bf16[768,768]{1,0:T(8,128)(2,1)S(1)}, bf16[768,768]{1,0:T(8,128)(2,1)S(1)}, bf16[768,768]{1,0:T(8,128)(2,1)S(1)}, f32[6,8,512]{2,1,0:T(8,128)S(1)}) custom-call(s32[3]{0:T(128)S(1)} %copy-done.16, bf16[768,768]{1,0:T(8,128)(2,1)S(1)} %convolution_convert_fusion.10.q_ref, bf16[768,768]{1,0:T(8,128)(2,1)S(1)} %copy-done.4, ...), custom_call_target="tpu_custom_call" | custom-call | tf_op jit(solution)/shard_map/attn_bwd/pallas_call | solution.py:155
  427.8 2.1 convolution_convert_fusion.6
  430.0 3.8 convolution_convert_fusion.5
  433.9 3.5 convolution_convert_fusion.4
  437.5 4.2 convolution_convert_fusion.3
  441.7 6.6 convolution_convert_fusion.2
  448.4 6.6 convolution_convert_fusion.1
  455.1 6.5 convolution_convert_fusion
  466.5 2.2 multiply_reduce_fusion.1
  470.4 11.7 %gbst_bwd.1 = (f32[272,768]{1,0:T(8,128)S(1)}, f32[1,768]{1,0:T(1,128)S(1)}) custom-call(s32[3]{0:T(128)S(1)} %copy-done.16, s32[16,128]{1,0:T(8,128)S(1)} %pad.12.ids_ref, bf16[1536,768]{1,0:T(8,128)(2,1)S(1)} %copy-done.5, f32[128,128]{1,0:T(8,128)S(1)} %copy-done.12, bf16[1,768]{1,0:T(2,128)(2,1)S(1)} %broadcast_in_dim.6.score_ref, ...), custom_call_target="tpu_custom_call" | custom-call | tf_op jit(solution)/shard_map/gbst_bwd/pallas_call | solution.py:379
  485.3 40.0 %all-reduce.6 = (f32[768]{0:T(1024)S(1)}, f32[768]{0:T(1024)S(1)}, f32[32,12]{0,1:T(8,128)}, f32[768]{0:T(1024)S(1)}, f32[5]{0:T(128)S(1)}) all-reduce(f32[768]{0:T(1024)S(1)} %reduce.1, f32[768]{0:T(1024)S(1)} %copy-done.43, f32[32,12]{0,1:T(8,128)S(1)} %fusion.15, ...), channel_id=1, replica_groups=mesh['wide'=8,'narrow'=4] {'wide','narrow'}, use_global_device_ids=true, to_apply=%region_6.7 | all-reduce | flops 2693 | bytes 21544 | tf_op jit(solution)/shard_map/psum | solution.py:466
  528.7 30.5 %reduce-scatter.13.cloned.1.call-done = bf16[96,768]{1,0:T(8,128)(2,1)} async-done(((bf16[768,768]{1,0:T(8,128)(2,1)}), bf16[96,768]{1,0:T(8,128)(2,1)}) %reduce-scatter.13.cloned.1.call-update) | async-done | bytes 147472 | tf_op jit(solution)/shard_map/reduce_scatter | solution.py:464
  559.2 66.3 %reduce-scatter.15.cloned.1.call-done = bf16[96,768]{1,0:T(8,128)(2,1)} async-done(((bf16[768,768]{1,0:T(8,128)(2,1)}), bf16[96,768]{1,0:T(8,128)(2,1)}) %reduce-scatter.15.cloned.1.call-update) | async-done | bytes 147472 | tf_op jit(solution)/shard_map/reduce_scatter | solution.py:464
  625.5 66.6 %reduce-scatter.17.cloned.1.call-done = bf16[96,768]{1,0:T(8,128)(2,1)} async-done(((bf16[768,768]{1,0:T(8,128)(2,1)}), bf16[96,768]{1,0:T(8,128)(2,1)}) %reduce-scatter.17.cloned.1.call-update) | async-done | bytes 147472 | tf_op jit(solution)/shard_map/reduce_scatter | solution.py:464
  692.1 76.7 %reduce-scatter.19.cloned.1.call-done = bf16[96,2048]{1,0:T(8,128)(2,1)} async-done(((bf16[768,2048]{1,0:T(8,128)(2,1)}), bf16[96,2048]{1,0:T(8,128)(2,1)}) %reduce-scatter.19.cloned.1.call-update) | async-done | bytes 393232 | tf_op jit(solution)/shard_map/reduce_scatter | solution.py:464
  768.9 77.3 %reduce-scatter.21.cloned.1.call-done = bf16[96,2048]{1,0:T(8,128)(2,1)} async-done(((bf16[768,2048]{1,0:T(8,128)(2,1)}), bf16[96,2048]{1,0:T(8,128)(2,1)}) %reduce-scatter.21.cloned.1.call-update) | async-done | bytes 393232 | tf_op jit(solution)/shard_map/reduce_scatter | solution.py:464
  846.1 76.9 %reduce-scatter.23.cloned.1.call-done = bf16[256,768]{1,0:T(8,128)(2,1)} async-done(((bf16[2048,768]{1,0:T(8,128)(2,1)}), bf16[256,768]{1,0:T(8,128)(2,1)}) %reduce-scatter.23.cloned.1.call-update) | async-done | bytes 393232 | tf_op jit(solution)/shard_map/reduce_scatter | solution.py:464
  923.1 5.6 fusion.37
  928.7 1.2 fusion.9
  929.9 58.1 %reduce-scatter.25.cloned.1.call-done = bf16[96,259]{1,0:T(8,128)(2,1)} async-done(((bf16[768,259]{1,0:T(8,128)(2,1)}), bf16[96,259]{1,0:T(8,128)(2,1)}) %reduce-scatter.25.cloned.1.call-update) | async-done | bytes 49744
  989.1 11.8 %psum.91 = bf16[259,96]{1,0:T(8,128)(2,1)S(1)} all-reduce(bf16[259,96]{1,0:T(8,128)(2,1)S(1)} %copy.36), channel_id=1, replica_groups=mesh['wide'=8,'narrow'=4] {'narrow'}, use_global_device_ids=true, to_apply=%region_5.6 | all-reduce | flops 24864 | bytes 99456 | tf_op jit(solution)/shard_map/psum | solution.py:465
  1001.5 36.0 %all-reduce.11.cloned.1.call-done = (bf16[96,768]{1,0:T(8,128)(2,1)}, bf16[96,768]{1,0:T(8,128)(2,1)}, bf16[96,768]{1,0:T(8,128)(2,1)}, bf16[96,768]{1,0:T(8,128...) async-done(((bf16[96,768]{1,0:T(8,128)(2,1)}, bf16[96,768]{1,0:T(8,128)(2,1)}, bf16[96,768]{1,0:T(8,128)(2,1)}, ...) | async-done | bytes 1769488 | tf_op jit(solution)/shard_map/psum | solution.py:465
  1037.5 2.0 convert_element_type.229
  1039.5 1.9 convert_element_type.231
  (188 shorter events, 42.0 us)
Async XLA Ops:
  7.2 80.8 %copy-start = (bf16[32,12]{0,1:T(8,128)(2,1)S(1)}, bf16[32,12]{0,1:T(8,128)(2,1)}, u32[]{:S(2)}) copy-start(bf16[32,12]{0,1:T(8,128)(2,1)} %param.27) | copy-start | bytes 2308
  7.2 81.6 %all-gather.9.cloned.1.call-start = ((), (), s32[]{:S(2)}) async-start(), calls=%async_computation.8 | async-start | bytes 1327104 | tf_op jit(solution)/shard_map/all_gather | solution.py:457
  7.9 92.2 %all-gather.13.cloned.1.call-start = ((), (), s32[]{:S(2)}) async-start(), calls=%async_computation.10 | async-start | bytes 1327104 | tf_op jit(solution)/shard_map/all_gather | solution.py:457
  8.7 133.5 %all-gather.11.cloned.1.call-start = ((), (), s32[]{:S(2)}) async-start(), calls=%async_computation.9 | async-start | bytes 1327104 | tf_op jit(solution)/shard_map/all_gather | solution.py:457
  9.4 174.7 %all-gather.15.cloned.1.call-start = ((), (), s32[]{:S(2)}) async-start(), calls=%async_computation.11 | async-start | bytes 1327104 | tf_op jit(solution)/shard_map/all_gather | solution.py:457
  10.0 235.4 %all-gather.17.cloned.1.call-start = ((), (), s32[]{:S(2)}) async-start(), calls=%async_computation.12 | async-start | bytes 3538944 | tf_op jit(solution)/shard_map/all_gather | solution.py:457
  10.6 63.9 %copy-start.46 = (s32[1,2]{1,0:T(1,128)S(1)}, s32[1,2]{1,0:T(1,128)}, u32[]{:S(2)}) copy-start(s32[1,2]{1,0:T(1,128)} %param.17) | copy-start | bytes 28
  10.6 295.9 %all-gather.19.cloned.1.call-start = ((), (), s32[]{:S(2)}) async-start(), calls=%async_computation.13 | async-start | bytes 3538944 | tf_op jit(solution)/shard_map/all_gather | solution.py:457
  11.2 356.7 %all-gather.21.cloned.1.call-start = ((), (), s32[]{:S(2)}) async-start(), calls=%async_computation.14 | async-start | bytes 3538944 | tf_op jit(solution)/shard_map/all_gather | solution.py:457
  11.9 516.8 %reduce-scatter.11.cloned.1.call-start = ((), (), s32[]{:S(2)}) async-start(), calls=%async_computation.15 | async-start | bytes 1327104 | tf_op jit(solution)/shard_map/reduce_scatter | solution.py:464
  76.4 9.3 copy-start.15
  103.9 41.1 %copy-start.16 = (s32[3]{0:T(128)S(1)}, s32[3]{0:T(128)}, u32[]{:S(2)}) copy-start(s32[3]{0:T(128)} %copy-done.15) | copy-start | bytes 40
  142.2 2.8 copy-start.2
  142.2 2.8 copy-start.9
  184.1 4.2 copy-start.40
  367.8 12.9 %copy-start.47 = (bf16[768,2048]{1,0:T(8,128)(2,1)S(1)}, bf16[768,2048]{1,0:T(8,128)(2,1)}, u32[]{:S(2)}) copy-start(bf16[768,2048]{1,0:T(8,128)(2,1)} %all-gather.17.cloned.1.call-done) | copy-start | bytes 9437188
  380.7 2.7 copy-start.52
  380.7 3.2 copy-start.51
  380.7 3.4 copy-start.26
  380.7 3.4 copy-start.39
  380.8 3.4 copy-start.41
  380.8 4.9 copy-start.48
  385.6 3.5 copy-start.32
  385.6 3.5 copy-start.42
  390.4 2.2 copy-start.28
  390.4 2.2 copy-start.4
  390.4 2.2 copy-start.10
  390.5 2.2 copy-start.14
  392.6 35.1 %copy-start.19 = (bf16[768,768]{1,0:T(8,128)(2,1)S(1)}, bf16[768,768]{1,0:T(8,128)(2,1)}, u32[]{:S(2)}) copy-start(bf16[768,768]{1,0:T(8,128)(2,1)} %copy-done.18) | copy-start | bytes 3538948
  430.0 129.3 %reduce-scatter.13.cloned.1.call-start = ((), (), s32[]{:S(2)}) async-start(), calls=%async_computation.16 | async-start | bytes 1327104 | tf_op jit(solution)/shard_map/reduce_scatter | solution.py:464
  430.0 3.9 copy-start.7
  433.9 191.6 %reduce-scatter.15.cloned.1.call-start = ((), (), s32[]{:S(2)}) async-start(), calls=%async_computation.17 | async-start | bytes 1327104 | tf_op jit(solution)/shard_map/reduce_scatter | solution.py:464
  437.4 254.7 %reduce-scatter.17.cloned.1.call-start = ((), (), s32[]{:S(2)}) async-start(), calls=%async_computation.18 | async-start | bytes 1327104 | tf_op jit(solution)/shard_map/reduce_scatter | solution.py:464
  441.7 327.2 %reduce-scatter.19.cloned.1.call-start = ((), (), s32[]{:S(2)}) async-start(), calls=%async_computation.19 | async-start | bytes 3538944 | tf_op jit(solution)/shard_map/reduce_scatter | solution.py:464
  448.4 397.7 %reduce-scatter.21.cloned.1.call-start = ((), (), s32[]{:S(2)}) async-start(), calls=%async_computation.20 | async-start | bytes 3538944 | tf_op jit(solution)/shard_map/reduce_scatter | solution.py:464
  455.1 468.0 %reduce-scatter.23.cloned.1.call-start = ((), (), s32[]{:S(2)}) async-start(), calls=%async_computation.21 | async-start | bytes 3538944 | tf_op jit(solution)/shard_map/reduce_scatter | solution.py:464
  461.7 526.4 %reduce-scatter.25.cloned.1.call-start = ((), (), s32[]{:S(2)}) async-start(), calls=%async_computation.22 | async-start | bytes 663552
  466.5 2.2 copy-start.29
  482.1 3.2 copy-start.43
  482.1 3.2 copy-start.45
  483.3 554.2 %all-reduce.11.cloned.1.call-start = ((), (), s32[]{:S(2)}) async-start(), calls=%async_computation.23 | async-start | bytes 3538944 | tf_op jit(solution)/shard_map/psum | solution.py:465
  923.1 5.6 copy-start.27
  1037.5 4.0 copy-start.33
  1037.5 4.9 copy-start.37
  1037.5 5.7 copy-start.36
  1037.5 6.4 copy-start.35
  1037.5 7.1 copy-start.34
  1037.5 7.9 copy-start.1
  (21 other events, 23.4 us)
Sparse Core Ops, SparseCore 0:
  10.2 46.4 all-gather.8
  58.9 41.2 all-gather.12
  102.3 39.8 all-gather.10
  144.2 39.8 all-gather.14
  186.1 59.2 all-gather.16
  247.4 59.0 all-gather.18
  308.7 59.0 all-gather.20
  430.1 62.6 reduce-scatter.10
  496.2 63.0 reduce-scatter.12
  562.4 63.0 reduce-scatter.14
  628.9 63.1 reduce-scatter.16
  695.6 73.2 reduce-scatter.18
  772.4 73.6 reduce-scatter.20
  849.6 73.4 reduce-scatter.22
  926.8 61.2 reduce-scatter.24
  991.0 46.3 all-reduce.10
